TPU v7x, 256 devices: a whole 4x4x8 slice. The times are simulated.
256 devices in a mesh: blk: 32 (over y_lo, z, core), uly: 8 (over y_hi, x).
Axes of the slice: x: 4, y: 4 (y_hi: 2, y_lo: 2; y = y_hi * 2 + y_lo), z: 8, core: 2. Of those that a mesh axis runs over, the one named last changes fastest.
Arguments:
- video_tokens: bfloat16 [8192, 3072], P(('blk', 'uly')), may hold values from -6 to 6
- w_qkv: bfloat16 [3072, 9216], P(None, 'uly'), may hold values from -0.109375 to 0.109375
- w_out: bfloat16 [3072, 3072], P('uly'), may hold values from -0.109375 to 0.109375
- text_tokens: bfloat16 [256, 3072], P(None, 'blk'), may hold values from -6 to 6
- w_text: bfloat16 [3072, 6144], P('blk', 'uly'), may hold values from -0.109375 to 0.109375
- q_gain: float32 [128], replicated, may hold values from 1.5 to 5.5
- k_gain: float32 [128], replicated, may hold values from 1.5 to 5.5
- text_gain: float32 [128], replicated, may hold values from 1.5 to 5.5
Outputs:
- video_out: bfloat16 [8192, 3072], P(('blk', 'uly'))
All inputs are finite; a program needn't handle non-finite values.
Results may differ from a plain program's by a relative error of at most 0.018.
The roundings to bfloat16 on the way count: a program that leaves them out, or rounds other values in their place, can miss the bound.
Values may be sent and summed in bfloat16 or wider, within the bound.
A program may use at most 128 MiB of HBM per device.

v0:
```python
import math

import jax
import jax.numpy as jnp
from jax import lax
from jax.sharding import PartitionSpec as P

HD = 128


def normed(values, gains):
    factor = lax.rsqrt(jnp.mean(values * values, axis=-1, keepdims=True) + 1e-06)
    return values * factor * gains


def attend(running, key_block, value_block, queries, score_scale):
    row_peak, row_total, blended = running
    scores = (
        jnp.einsum("qhd,khd->qhk", queries, key_block, preferred_element_type=jnp.float32)
        * score_scale
    )
    new_peak = jnp.maximum(row_peak, jnp.max(scores, axis=-1))
    shrink = jnp.exp(row_peak - new_peak)
    weights = jnp.exp(scores - new_peak[..., None])
    row_total = row_total * shrink + jnp.sum(weights, axis=-1)
    blended = blended * shrink[..., None] + jnp.einsum(
        "qhk,khd->qhd",
        weights.astype(jnp.bfloat16),
        value_block,
        preferred_element_type=jnp.float32,
    )
    return (new_peak, row_total, blended)


def per_device(video_tokens, w_qkv, w_out, text_tokens, w_text, q_gain, k_gain, text_gain):
    projected = jnp.dot(
        lax.all_gather(video_tokens, "uly", axis=0, tiled=True),
        w_qkv,
        preferred_element_type=jnp.float32,
    )
    block_rows = projected.shape[0]
    local_heads = w_qkv.shape[1] // (3 * HD)
    projected = projected.reshape(block_rows, local_heads, 3, HD)
    queries = normed(projected[:, :, 0], q_gain).astype(jnp.bfloat16)
    video_keys = normed(projected[:, :, 1], k_gain).astype(jnp.bfloat16)
    video_values = projected[:, :, 2].astype(jnp.bfloat16)
    full_text, full_weight = (
        lax.all_gather(text_tokens, "blk", axis=1, tiled=True),
        lax.all_gather(w_text, "blk", axis=0, tiled=True),
    )
    text_projected = jnp.dot(full_text, full_weight, preferred_element_type=jnp.float32)
    text_projected = text_projected.reshape(text_tokens.shape[0], local_heads, 2, HD)
    text_keys = normed(text_projected[:, :, 0], text_gain).astype(jnp.bfloat16)
    text_values = text_projected[:, :, 1].astype(jnp.bfloat16)
    score_scale = HD ** (-0.5)
    text_scores = (
        jnp.einsum("qhd,khd->qhk", queries, text_keys, preferred_element_type=jnp.float32)
        * score_scale
    )
    first_peak = jnp.max(text_scores, axis=-1)
    text_weights = jnp.exp(text_scores - first_peak[..., None])
    first_total = jnp.sum(text_weights, axis=-1)
    first_blend = jnp.einsum(
        "qhk,khd->qhd",
        text_weights.astype(jnp.bfloat16),
        text_values,
        preferred_element_type=jnp.float32,
    )
    starting = (first_peak, first_total, first_blend)
    running = starting
    key_rows = lax.all_gather(video_keys, "blk", axis=0, tiled=True)
    value_rows = lax.all_gather(video_values, "blk", axis=0, tiled=True)
    shard_count = key_rows.shape[0] // block_rows
    per_step = math.gcd(shard_count, max(1, 2048 // block_rows))
    step_rows = per_step * block_rows
    stacked_keys = key_rows.reshape(shard_count // per_step, step_rows, local_heads, HD)
    stacked_values = value_rows.reshape(shard_count // per_step, step_rows, local_heads, HD)

    def step_blocks(inner_state, blocks):
        return (attend(inner_state, blocks[0], blocks[1], queries, score_scale), None)

    running, unused = lax.scan(step_blocks, running, (stacked_keys, stacked_values))
    final_peak, final_total, final_blend = running
    attended = (
        (final_blend / final_total[..., None])
        .astype(jnp.bfloat16)
        .reshape(block_rows, local_heads * HD)
    )
    return lax.psum_scatter(
        jnp.dot(attended, w_out, preferred_element_type=jnp.float32).astype(jnp.bfloat16),
        "uly",
        scatter_dimension=0,
        tiled=True,
    )


def solution(mesh):
    in_specs = (
        P(("blk", "uly"), None),
        P(None, "uly"),
        P("uly", None),
        P(None, "blk"),
        P("blk", "uly"),
        P(),
        P(),
        P(),
    )
    out_specs = P(("blk", "uly"), None)
    return jax.shard_map(
        per_device, mesh=mesh, in_specs=in_specs, out_specs=out_specs, check_vma=False
    )
```

profile of v0, /device:TPU:1, one launch (start us, length us, event | category | flops | bytes accessed | tf_op | source)
XLA Modules:
  0.0 469.0 jit_solution(7286811275066480799)
XLA Ops:
  8.8 59.7 %all-gather.11.cloned.1.call-done = bf16[256,3072]{1,0:T(8,128)(2,1)} async-done(((bf16[32,3072]{1,0:T(8,128)(2,1)}), bf16[256,3072]{1,0:T(8,128)(2,1)}) %all-gather.11.cloned.1.call-update) | async-done | bytes 1572880 | tf_op jit(solution)/shard_map/all_gather | solution.py:37
  68.6 6.3 %fusion.39 = f32[256,1152]{0,1:T(8,128)S(1)} fusion(bf16[256,3072]{1,0:T(8,128)(2,1)} %all-gather.11.cloned.1.call-done, bf16[3072,1152]{1,0:T(8,128)(2,1)} %param.11), kind=kOutput, calls=%fused_computation.50 | convolution fusion | flops 1811939328 | bytes 9830400 | tf_op jit(solution)/shard_map/dot_general | solution.py:36
  76.8 1.1 copy.21
  81.4 54.2 %all-gather.7.cloned.1.call-done = bf16[256,3072]{0,1:T(8,128)(2,1)} async-done(((bf16[256,96]{0,1:T(8,128)(2,1)}), bf16[256,3072]{0,1:T(8,128)(2,1)}) %all-gather.7.cloned.1.call-update) | async-done | bytes 1572880 | tf_op jit(solution)/shard_map/all_gather | solution.py:48
  135.6 69.5 %all-gather.9.cloned.1.call-done = bf16[3072,768]{1,0:T(8,128)(2,1)} async-done(((bf16[96,768]{1,0:T(8,128)(2,1)}), bf16[3072,768]{1,0:T(8,128)(2,1)}) %all-gather.9.cloned.1.call-update) | async-done | bytes 4718608 | tf_op jit(solution)/shard_map/all_gather | solution.py:49
  205.1 5.1 %fusion.38 = f32[256,768]{1,0:T(8,128)} fusion(bf16[256,3072]{0,1:T(8,128)(2,1)} %all-gather.7.cloned.1.call-done, bf16[3072,768]{1,0:T(8,128)(2,1)} %all-gather.9.cloned.1.call-done), kind=kOutput, calls=%fused_computation.49 | convolution fusion | flops 1207959552 | bytes 7077888 | tf_op jit(solution)/shard_map/dot_general | solution.py:51
  210.3 2.4 reshape.48
  212.7 1.4 slice.22
  214.1 1.5 slice.24
  217.3 1.2 convolution_bitcast_fusion
  218.5 68.3 %all-gather.15.cloned.1.call-done = bf16[8192,3,1,128]{0,3,2,1:T(8,128)(2,1)} async-done(((bf16[256,3,1,128]{0,3,2,1:T(8,128)(2,1)}), bf16[8192,3,1,128]{0,3,2,1:T(8,128)(2,1)}) %all-gather.15.cloned.1.call-update) | async-done | bytes 6291472 | tf_op jit(solution)/shard_map/all_gather | solution.py:72
  286.8 8.7 %copy.22 = bf16[8192,3,1,128]{3,0,1,2:T(8,128)(2,1)} copy(bf16[8192,3,1,128]{0,3,2,1:T(8,128)(2,1)} %all-gather.15.cloned.1.call-done) | data formatting | bytes 12582912 | tf_op jit(solution)/shard_map/all_gather | solution.py:72
  295.4 61.5 %all-gather.13.cloned.1.call-done = bf16[8192,3,128]{2,0,1:T(8,128)(2,1)} async-done(((bf16[256,3,128]{2,0,1:T(8,128)(2,1)}), bf16[8192,3,128]{2,0,1:T(8,128)(2,1)}) %all-gather.13.cloned.1.call-update) | async-done | bytes 6291472 | tf_op jit(solution)/shard_map/all_gather | solution.py:71
  356.9 25.2 %while.14 = (s32[]{:T(128)}, f32[256,3]{0,1:T(4,128)S(1)}, f32[256,3]{0,1:T(4,128)S(1)}, f32[256,3,128]{0,2,1:T(8,128)S(1)}, bf16[4,2048,3,128]{3,1,0,2:T(8,128)...) while((s32[]{:T(128)}, f32[256,3]{0,1:T(4,128)S(1)}, ...), condition=%wide.region_8.9_spmd, body=%wide.region_5.8_spmd.sunk | while | flops 818087424 | bytes 23053396 | solution.py:82
  356.9 2.4 bitcast_reduce_fusion.2
  360.4 2.8 fusion.57
  363.2 2.4 bitcast_reduce_fusion.2
  366.7 2.8 fusion.57
  369.5 2.4 bitcast_reduce_fusion.2
  373.0 2.8 fusion.57
  375.9 2.4 bitcast_reduce_fusion.2
  379.3 2.8 fusion.57
  382.2 2.2 convolution_convert_fusion
  384.4 77.8 %reduce-scatter.2.cloned.1.call-done = bf16[32,3072]{1,0:T(8,128)(2,1)} async-done(((bf16[256,3072]{1,0:T(8,128)(2,1)}), bf16[32,3072]{1,0:T(8,128)(2,1)}) %reduce-scatter.2.cloned.1.call-update) | async-done | bytes 196624 | tf_op jit(solution)/shard_map/reduce_scatter | solution.py:89
  (53 shorter events, 13.3 us)
Async XLA Ops:
  6.5 375.7 %copy-start = (bf16[384,3072]{1,0:T(8,128)(2,1)S(1)}, bf16[384,3072]{1,0:T(8,128)(2,1)}, u32[]{:S(2)}) copy-start(bf16[384,3072]{1,0:T(8,128)(2,1)} %param.12) | copy-start | bytes 7077892
  6.5 62.0 %all-gather.11.cloned.1.call-start = ((), (), s32[]{:S(2)}) async-start(), calls=%async_computation.3 | async-start | bytes 1769472 | tf_op jit(solution)/shard_map/all_gather | solution.py:37
  7.3 128.3 %all-gather.7.cloned.1.call-start = ((), (), s32[]{:S(2)}) async-start(), calls=%async_computation.1 | async-start | bytes 1622016 | tf_op jit(solution)/shard_map/all_gather | solution.py:48
  8.0 197.1 %all-gather.9.cloned.1.call-start = ((), (), s32[]{:S(2)}) async-start(), calls=%async_computation.2 | async-start | bytes 4866048 | tf_op jit(solution)/shard_map/all_gather | solution.py:49
  8.7 69.4 %copy-start.3 = (f32[128]{0:T(128)S(1)}, f32[128]{0:T(128)}, u32[]{:S(2)}) copy-start(f32[128]{0:T(128)} %param.16) | copy-start | bytes 1540
  8.8 71.4 %copy-start.4 = (f32[128]{0:T(128)S(1)}, f32[128]{0:T(128)}, u32[]{:S(2)}) copy-start(f32[128]{0:T(128)} %param.15) | copy-start | bytes 1540
  8.8 278.0 %all-gather.15.cloned.1.call-start = ((), (), s32[]{:S(2)}) async-start(), calls=%async_computation.6 | async-start | bytes 6488064 | tf_op jit(solution)/shard_map/all_gather | solution.py:72
  74.9 1.1 copy-start.1
  75.7 281.2 %all-gather.13.cloned.1.call-start = ((), (), s32[]{:S(2)}) async-start(), calls=%async_computation.4 | async-start | bytes 6488064 | tf_op jit(solution)/shard_map/all_gather | solution.py:71
  79.0 383.2 %reduce-scatter.2.cloned.1.call-start = ((), (), s32[]{:S(2)}) async-start(), calls=%async_computation.5 | async-start | bytes 1769472 | tf_op jit(solution)/shard_map/reduce_scatter | solution.py:89
  81.4 135.4 %copy-start.2 = (f32[128]{0:T(128)S(1)}, f32[128]{0:T(128)}, u32[]{:S(2)}) copy-start(f32[128]{0:T(128)} %param.17) | copy-start | bytes 1540
Sparse Core Ops, SparseCore 0:
  10.0 58.5 all-gather.10
  70.4 65.1 all-gather.6
  137.4 67.6 all-gather.8
  206.7 79.9 all-gather.14
  288.5 68.3 all-gather.12
  384.5 77.5 reduce-scatter.1
where the time goes:
time: 470 us; the launch traced here: 469 us
  waiting for transfers between devices  393 us (84%)
  matrix products  36 us (8%)
  local copies, waits for them, and re-layouts  18.1 us (4%)
  between operations  13.6 us (3%)
  other arithmetic  7.78 us (2%)
    reduce_scatter x1, waiting for transfers between devices, per_device(): lax.psum_scatter(jnp.dot(attended, w_out, preferred_element_type=jnp.floa...  77.8 us
    all_gather x1, waiting for transfers between devices, per_device(): lax.all_gather(w_text, 'blk', axis=0, tiled=True)  69.5 us
    all_gather x1, waiting for transfers between devices, per_device(): value_rows = lax.all_gather(video_values, 'blk', axis=0, tiled=True)  68.3 us
    all_gather x1, waiting for transfers between devices, per_device(): key_rows = lax.all_gather(video_keys, 'blk', axis=0, tiled=True)  61.5 us
    all_gather x1, waiting for transfers between devices, per_device(): lax.all_gather(video_tokens, 'uly', axis=0, tiled=True)  59.7 us
    all_gather x1, waiting for transfers between devices, per_device(): lax.all_gather(text_tokens, 'blk', axis=1, tiled=True)  54.2 us
    dot_general x4, matrix products, attend(): jnp.einsum('qhk,khd->qhd', weights.astype(jnp.bfloat16), value_block, pre...  11.2 us
    dot_general x4, matrix products, attend(): jnp.einsum('qhd,khd->qhk', queries, key_block, preferred_element_type=jnp...  9.61 us
  transfers between devices with their start and end apart: 6, of which 6 were waited for; matrix products, arithmetic and copies ran while one was open for 7% of the time, Pallas kernels for 0%

commit v1 on v0

v1 whole, which is shorter than its diff:
```python
import functools
import math

import jax
import jax.numpy as jnp
from jax import lax
from jax.experimental import pallas as pl
from jax.experimental.pallas import tpu as pltpu
from jax.sharding import PartitionSpec as P

MESH = pl.DeviceIdType.MESH
HD = 128
NH = 3
D = 3072
TEXT = 256
ROWS = 32
HALF = 16
CHUNK = 128
NZ, NX = 8, 4
SCALE2 = HD ** (-0.5) * math.log2(math.e)
BF16, F32 = jnp.bfloat16, jnp.float32


class Sems:
    def __init__(self, send, recv):
        self.send, self.recv, self.at = send, recv, {}

    def __call__(self, *name):
        index = self.at.setdefault(name, len(self.at))
        return {"send_sem": self.send.at[index], "recv_sem": self.recv.at[index]}


N_SEMS = 96


def normed(values, gains):
    factor = lax.rsqrt(jnp.mean(values * values, axis=-1, keepdims=True) + 1e-06)
    return values * factor * gains


def kernel(
    tok_hbm, wq_hbm, wo_hbm, tt_ref, wt_ref, qg_ref, kg_ref, tg_ref, out_ref,
    tok, relay, wq, wo, kv, q, acc, top, total,
    tpart, tcr, tsum, tyr, tsum2, tzr, tkv,
    osend, orecv, ssend, srecv, part, rsrecv,
    send_sems, recv_sems, local_sems,
):
    b, u = lax.axis_index("blk"), lax.axis_index("uly")
    y_lo, z, c = b // 16, (b // 2) % NZ, b % 2
    y_hi, x = u // NX, u % NX
    y = 2 * y_hi + y_lo
    sems = Sems(send_sems, recv_sems)
    pending = []

    def device(y_lo=y_lo, z=z, c=c, y_hi=y_hi, x=x):
        return {"blk": (y_lo * NZ + z) * 2 + c, "uly": y_hi * NX + x}

    def y_step(k):
        yy = (y + k) % 4
        return device(y_hi=yy // 2, y_lo=yy % 2)

    def x_step(k):
        return device(x=(x + k) % NX)

    def z_step(k):
        return device(z=(z + k) % NZ)

    sibling = device(c=1 - c)
    partner = device(y_lo=1 - y_lo)

    def send(name, src, dst, where):
        copy = pltpu.make_async_remote_copy(
            src_ref=src, dst_ref=dst, device_id=where, device_id_type=MESH, **sems(*name)
        )
        copy.start()
        pending.append(copy)

    def wait(name, dst):
        pltpu.make_async_remote_copy(
            src_ref=dst, dst_ref=dst, device_id=sibling, device_id_type=MESH, **sems(*name)
        ).wait_recv()

    barrier = pltpu.get_barrier_semaphore()
    peers = [device(z=(z + dz) % NZ, c=(c + dc) % 2) for dz in range(NZ) for dc in range(2) if dz or dc]
    peers += [y_step(1), y_step(-1)]
    peers += [device(y_hi=(y_hi + j) % 2, x=(x + dx) % NX) for j in range(2) for dx in range(NX) if j or dx]
    for peer in peers:
        pl.semaphore_signal(barrier, inc=1, device_id=peer, device_id_type=MESH)
    pl.semaphore_wait(barrier, len(peers))

    def rows(start, size, step):
        return pl.ds(pl.multiple_of(start * step, step), size)

    def slot(j, dx, first=0, size=ROWS):
        start = ((x + dx) % NX) * ROWS + first
        return tok.at[(y_hi + j) % 2, pl.ds(pl.multiple_of(start, HALF), size), :]

    local_tok = pltpu.make_async_copy(tok_hbm, slot(0, 0), local_sems.at[0])
    local_wq = pltpu.make_async_copy(wq_hbm, wq, local_sems.at[1])
    local_wo = pltpu.make_async_copy(wo_hbm, wo, local_sems.at[2])

    send(("x", 0, 1), tok_hbm, slot(0, 0), x_step(1))
    send(("x", 0, -1), tok_hbm, slot(0, 0), x_step(-1))
    for k, first in ((1, 0), (-1, HALF)):
        send(("y", k), tok_hbm.at[pl.ds(first, HALF), :], relay.at[first // HALF], y_step(k))
    local_tok.start()
    local_wq.start()
    local_wo.start()

    product = jnp.dot(tt_ref[...], wt_ref[...], preferred_element_type=F32)
    for h in range(NH):
        for s in range(2):
            at = (2 * h + s) * HD
            tpart[s, :, h * HD:(h + 1) * HD] = product[:, at:at + HD]
    send(("tc",), tpart.at[1 - c], tcr, sibling)

    for k, first in ((1, 0), (-1, HALF)):
        wait(("y", k), relay.at[first // HALF])
        source = (y - k) % 4
        dst = tok.at[source // 2, pl.ds(pl.multiple_of(x * ROWS + first, HALF), HALF), :]
        send(("yy", k), relay.at[first // HALF], dst, y_step(k))

    def pass_on(j):
        for k, first in ((1, 0), (-1, HALF)):
            wait(("x", j, k), slot(j, -k))
            send(("xx", j, k), slot(j, -k, first, HALF), slot(j, -k, first, HALF), x_step(k))

    pass_on(0)

    wait(("tc",), tcr)
    tsum[...] = tpart[c] + tcr[...]
    send(("ty",), tsum.at[rows(1 - y_lo, CHUNK, CHUNK), :], tyr, partner)

    for k, first in ((1, 0), (-1, HALF)):
        wait(("yy", k), slot(1, 0, first, HALF))
    send(("x", 1, 1), slot(1, 0), slot(1, 0), x_step(1))
    send(("x", 1, -1), slot(1, 0), slot(1, 0), x_step(-1))

    def project(j):
        for k, first in ((1, 0), (-1, HALF)):
            wait(("xx", j, k), slot(j, 2, first, HALF))
        mine = rows(c, CHUNK, CHUNK)

        @pl.loop(0, NH)
        def _(h):
            columns = pl.ds(pl.multiple_of(h * 3 * HD, HD), 3 * HD)
            r = jnp.dot(tok[(y_hi + j) % 2], wq[:, columns], preferred_element_type=F32)
            q[h, j * CHUNK:(j + 1) * CHUNK, :] = normed(r[:, :HD], qg_ref[...]).astype(BF16)
            kv[j, z, h, mine, :] = normed(r[:, HD:2 * HD], kg_ref[...]).astype(BF16)
            kv[j, z, NH + h, mine, :] = r[:, 2 * HD:].astype(BF16)

        block = kv.at[j, z, :, mine, :]
        send(("kv", j, 1, 1), block, block, z_step(1))
        send(("kv", j, -1, 1), block, block, z_step(-1))
        send(("sib", j, 0, 0), block, block, sibling)
        own, theirs = j * CHUNK, 2 * CHUNK + j * CHUNK
        send(("q", j), q.at[:, own:own + CHUNK, :], q.at[:, theirs:theirs + CHUNK, :], partner)

    def planes(h, k):
        if h < NZ // 2:
            return pl.ds(0, 2 * NH)
        return pl.ds(0 if k == 1 else NH, NH)

    def block_of(j, h, k, p, core):
        return kv.at[j, (z - k * h) % NZ, p, rows(core, CHUNK, CHUNK), :]

    def ring(j, h):
        for k in (1, -1):
            wait(("kv", j, k, h), block_of(j, h, k, planes(h, k), c))
            if h < NZ // 2:
                piece = block_of(j, h, k, planes(h + 1, k), c)
                send(("kv", j, k, h + 1), piece, piece, z_step(k))
        for k in (1, -1):
            piece = block_of(j, h, k, planes(h, k), c)
            send(("sib", j, h, k), piece, piece, sibling)

    def await_sibling(j, h):
        for k in (1, -1) if h else (0,):
            wait(("sib", j, h, k), block_of(j, h, k, planes(h, k) if h else pl.ds(0, 2 * NH), 1 - c))

    def attend(tiles):
        @pl.loop(0, 2)
        def _(t):
            at = rows(t, 2 * CHUNK, 2 * CHUNK)
            for h in range(NH):
                pairs = tiles(h)
                scores = []
                for keys, _ in pairs:
                    s = lax.dot_general(q[h, at, :], keys[...], (((1,), (1,)), ((), ())), preferred_element_type=F32)
                    scores.append([s[:, i:i + HD] for i in range(0, s.shape[1], HD)])
                peak = functools.reduce(jnp.maximum, [piece for s in scores for piece in s])
                old = top[h, at, :]
                new = jnp.maximum(old, jnp.max(peak, axis=1, keepdims=True))
                shrink = jnp.exp2((old - new) * SCALE2)
                weights = [[jnp.exp2((piece - new) * SCALE2) for piece in s] for s in scores]
                total[h, at, :] = total[h, at, :] * shrink + sum(piece for w in weights for piece in w)
                blended = acc[h, at, :] * shrink
                for w, (_, values) in zip(weights, pairs):
                    w = jnp.concatenate(w, axis=1).astype(BF16)
                    blended = blended + jnp.dot(w, values[...], preferred_element_type=F32)
                acc[h, at, :] = blended
                top[h, at, :] = new

    def video_tiles(*where):
        def tiles(h):
            return [(kv.at[j, zz, h], kv.at[j, zz, NH + h]) for j, zz in where]

        return tiles

    local_tok.wait()
    local_wq.wait()
    project(0)

    wait(("ty",), tyr)
    tsum2[...] = tsum[rows(y_lo, CHUNK, CHUNK), :] + tyr[...]
    for dz in range(1, NZ):
        target = (z + dz) % NZ
        send(("tz", dz), tsum2.at[rows(target, HALF, HALF), :], tzr.at[dz - 1], z_step(dz))

    pass_on(1)

    top[...] = jnp.full(top.shape, -1e30, F32)
    total[...] = jnp.zeros(total.shape, F32)
    acc[...] = jnp.zeros(acc.shape, F32)

    ring(0, 1)
    project(1)

    for dz in range(1, NZ):
        wait(("tz", dz), tzr.at[dz - 1])
    summed = tsum2[rows(z, HALF, HALF), :]
    for dz in range(1, NZ):
        summed = summed + tzr[dz - 1]
    for h in range(NH):
        one = summed[:, h * HD:(h + 1) * HD]
        one = jnp.where(c == 0, normed(one, tg_ref[...]), one)
        tkv[c * NH + h, rows(z, HALF, HALF), :] = one.astype(BF16)

    def text_piece(dz, dc):
        return tkv.at[pl.ds(((c + dc) % 2) * NH, NH), rows((z - dz) % NZ, HALF, HALF), :]

    others = [(dz, dc) for dz in range(NZ) for dc in range(2) if dz or dc]
    for dz, dc in others:
        send(("tg", dz, dc), text_piece(0, 0), text_piece(0, 0), device(z=(z + dz) % NZ, c=(c + dc) % 2))

    for j in range(2):
        theirs = 2 * CHUNK + j * CHUNK
        wait(("q", j), q.at[:, theirs:theirs + CHUNK, :])
    await_sibling(0, 0)
    await_sibling(1, 0)
    attend(video_tiles((0, z), (1, z)))

    def attend_far(j, h):
        await_sibling(j, h)
        attend(video_tiles((j, (z - h) % NZ), (j, (z + h) % NZ)))

    ring(1, 1)
    attend_far(0, 1)
    ring(0, 2)
    attend_far(1, 1)
    ring(1, 2)
    attend_far(0, 2)
    ring(0, 3)
    attend_far(1, 2)
    ring(1, 3)
    for dz, dc in others:
        wait(("tg", dz, dc), text_piece(dz, dc))
    attend(lambda h: [(tkv.at[h], tkv.at[NH + h])])
    attend_far(0, 3)
    ring(0, 4)
    attend_far(1, 3)
    ring(1, 4)
    await_sibling(0, 4)
    await_sibling(1, 4)
    attend(video_tiles((0, (z + 4) % NZ), (1, (z + 4) % NZ)))

    def finished(h, at):
        weight = jnp.sum(total[h, at, :], axis=1, keepdims=True)
        return acc[h, at, :] / weight, top[h, at, :] * SCALE2 + jnp.log2(weight)

    ssend[...] = jnp.zeros(ssend.shape, F32)
    for j in (1, 0):
        for h in range(NH):
            mean, level = finished(h, pl.ds(2 * CHUNK + j * CHUNK, CHUNK))
            osend[j, :, h * HD:(h + 1) * HD] = mean.astype(BF16)
            ssend[j, h:h + 1, :] = level.T[0:1, :]
        send(("s", j), ssend.at[j], srecv.at[j], partner)
        send(("o", j), osend.at[j], orecv.at[j], partner)

    local_wo.wait()
    for j in (1, 0):
        wait(("s", j), srecv.at[j])
        wait(("o", j), orecv.at[j])
        mixed = []
        for h in range(NH):
            mean, level = finished(h, pl.ds(j * CHUNK, CHUNK))
            other = jnp.broadcast_to(srecv[j, h:h + 1, :], (CHUNK, HD)).T
            peak = jnp.maximum(level, other)
            mine, theirs = jnp.exp2(level - peak), jnp.exp2(other - peak)
            both = mean * mine + orecv[j, :, h * HD:(h + 1) * HD].astype(F32) * theirs
            mixed.append((both / (mine + theirs)).astype(BF16))
        attended = jnp.concatenate(mixed, axis=1)
        for n in range(0, D, 512):
            r = jnp.dot(attended, wo[:, n:n + 512], preferred_element_type=F32)
            part[j, :, n:n + 512] = r.astype(BF16)
        for dx in (2, 1, 3, 0):
            if j or dx:
                where = device(y_hi=(y_hi + j) % 2, x=(x + dx) % NX)
                src = part.at[j, rows((x + dx) % NX, ROWS, ROWS), :]
                send(("rs", j, dx), src, rsrecv.at[j * NX + dx - 1], where)

    for j in (0, 1):
        for dx in range(NX):
            if j or dx:
                wait(("rs", j, dx), rsrecv.at[j * NX + dx - 1])

    for n in range(0, D, 512):
        out = part[0, rows(x, ROWS, ROWS), n:n + 512].astype(F32)
        for i in range(2 * NX - 1):
            out = out + rsrecv[i, :, n:n + 512].astype(F32)
        out_ref[:, n:n + 512] = out.astype(BF16)

    for copy in pending:
        copy.wait_send()


def per_device(video_tokens, w_qkv, w_out, text_tokens, w_text, q_gain, k_gain, text_gain):
    vmem, hbm = pl.BlockSpec(memory_space=pltpu.VMEM), pl.BlockSpec(memory_space=pl.ANY)
    return pl.pallas_call(
        kernel,
        out_shape=jax.ShapeDtypeStruct((ROWS, D), BF16),
        in_specs=[hbm, hbm, hbm] + [vmem] * 5,
        out_specs=vmem,
        scratch_shapes=[
            pltpu.VMEM((2, CHUNK, D), BF16),
            pltpu.VMEM((2, HALF, D), BF16),
            pltpu.VMEM((D, NH * 3 * HD), BF16),
            pltpu.VMEM((NH * HD, D), BF16),
            pltpu.VMEM((2, NZ, 2 * NH, 2 * CHUNK, HD), BF16),
            pltpu.VMEM((NH, 4 * CHUNK, HD), BF16),
            pltpu.VMEM((NH, 4 * CHUNK, HD), F32),
            pltpu.VMEM((NH, 4 * CHUNK, HD), F32),
            pltpu.VMEM((NH, 4 * CHUNK, HD), F32),
            pltpu.VMEM((2, TEXT, NH * HD), F32),
            pltpu.VMEM((TEXT, NH * HD), F32),
            pltpu.VMEM((TEXT, NH * HD), F32),
            pltpu.VMEM((CHUNK, NH * HD), F32),
            pltpu.VMEM((CHUNK, NH * HD), F32),
            pltpu.VMEM((NZ - 1, HALF, NH * HD), F32),
            pltpu.VMEM((2 * NH, CHUNK, HD), BF16),
            pltpu.VMEM((2, CHUNK, NH * HD), BF16),
            pltpu.VMEM((2, CHUNK, NH * HD), BF16),
            pltpu.VMEM((2, 8, HD), F32),
            pltpu.VMEM((2, 8, HD), F32),
            pltpu.VMEM((2, CHUNK, D), BF16),
            pltpu.VMEM((2 * NX - 1, ROWS, D), BF16),
            pltpu.SemaphoreType.DMA((N_SEMS,)),
            pltpu.SemaphoreType.DMA((N_SEMS,)),
            pltpu.SemaphoreType.DMA((3,)),
        ],
        compiler_params=pltpu.CompilerParams(
            collective_id=0, has_side_effects=True, vmem_limit_bytes=56 * 1024 * 1024
        ),
        name="joint_attention",
    )(
        video_tokens, w_qkv, w_out, text_tokens, w_text,
        q_gain.reshape(1, HD), k_gain.reshape(1, HD), text_gain.reshape(1, HD),
    )


def solution(mesh):
    in_specs = (
        P(("blk", "uly"), None), P(None, "uly"), P("uly", None), P(None, "blk"), P("blk", "uly"), P(), P(), P(),
    )
    return jax.shard_map(
        per_device, mesh=mesh, in_specs=in_specs, out_specs=P(("blk", "uly"), None), check_vma=False
    )
```

time: 470 us -> 102 us (0.22)
  waiting for transfers between devices: 393 us -> 0 us
  Pallas kernels: 0 us -> 99.1 us
  matrix products: 36 us -> 0 us
  local copies, waits for them, and re-layouts: 18.1 us -> 3.15 us
  between operations: 13.6 us -> 0.01 us
  other arithmetic: 7.78 us -> 0 us
    all_gather x5 -> x0, waiting for transfers between devices: 313 us -> none  [the longest x1 69.5 us: per_device(): lax.all_gather(w_text, 'blk', axis=0, tiled=True)]
    pallas_call x0 -> x1, Pallas kernels: none -> 99.1 us  [per_device(): pl.pallas_call(kernel, out_shape=jax.ShapeDtypeStruct((ROWS, D), BF16), i...]
    reduce_scatter x1 -> x0, waiting for transfers between devices: 77.8 us -> none  [per_device(): lax.psum_scatter(jnp.dot(attended, w_out, preferred_element_type=jnp.floa...]
    dot_general x13 -> x0, matrix products: 36 us -> none  [the longest x4 11.2 us: attend(): jnp.einsum('qhk,khd->qhd', weights.astype(jnp.bfloat16), value_block, pre...]
    all_gather x1 -> x0, local copies, waits for them, and re-layouts: 8.66 us -> none  [per_device(): value_rows = lax.all_gather(video_values, 'blk', axis=0, tiled=True)]
    reduce_sum x8 -> x0, other arithmetic: 5.7 us -> none  [the longest x4 4.15 us: attend(): row_total = row_total * shrink + jnp.sum(weights, axis=-1)]
    slice x5 -> x0, local copies, waits for them, and re-layouts: 5.64 us -> none  [the longest x2 1.93 us: per_device(): video_keys = normed(projected[:, :, 1], k_gain).astype(jnp.bfloat16)]
  transfers between devices with their start and end apart: 6 -> 0, of which waited for: 6 -> 0; matrix products, arithmetic and copies ran while one was open for 7% -> 0% of each run, Pallas kernels for 0% -> 0%
where the time goes in v1:
time: 102 us
  Pallas kernels  99.1 us (97%)
  local copies, waits for them, and re-layouts  3.15 us (3%)
    pallas_call x1, Pallas kernels, per_device(): pl.pallas_call(kernel, out_shape=jax.ShapeDtypeStruct((ROWS, D), BF16), i...  99.1 us
    unnamed x2, local copies, waits for them, and re-layouts  3.15 us

profile of v1, /device:TPU:1, one launch (start us, length us, event | category | flops | bytes accessed | tf_op | source)
XLA Modules:
  0.0 102.2 jit_solution(18017698396898974605)
XLA Ops:
  0.0 1.5 %copy.9.tt_ref = bf16[256,96]{1,0:T(8,128)(2,1)} copy(bf16[256,96]{0,1:T(8,128)(2,1)} %param.11) | data formatting | bytes 98304 | tf_op args[3]
  1.5 99.1 %joint_attention.1 = bf16[32,3072]{1,0:T(8,128)(2,1)} custom-call(bf16[32,3072]{1,0:T(8,128)(2,1)} %tok_hbm.1, bf16[3072,1152]{1,0:T(8,128)(2,1)} %wq_hbm.1, bf16[384,3072]{1,0:T(8,128)(2,1)} %wo_hbm.1, bf16[256,96]{1,0:T(8,128)(2,1)} %copy.9.tt_ref, bf16[96,768]{1,0:T(8,128)(2,1)} %wt_ref.1, f32[1,128]{1,0:T(1,128)} %bitcast.3, f32[1,128]{1,0:T(1,128)} %bitcast.4, ...), custom_call_target="tpu_custom_call" | custom-call | tf_op jit(solution)/shard_map/joint_attention/pallas_call | solution.py:329
  100.6 1.6 %copy.11 = bf16[32,3072]{1,0:T(8,128)(2,1)} copy(bf16[32,3072]{1,0:T(8,128)(2,1)} %joint_attention.1) | data formatting | bytes 393216

commit v2 on v1

v2 whole, which is shorter than its diff:
```python
import functools
import math

import jax
import jax.numpy as jnp
from jax import lax
from jax.experimental import pallas as pl
from jax.experimental.pallas import tpu as pltpu
from jax.sharding import PartitionSpec as P

MESH = pl.DeviceIdType.MESH
HD = 128
NH = 3
D = 3072
TEXT = 256
ROWS = 32
HALF = 16
CHUNK = 128
NZ, NX = 8, 4
COLS = D // 2
SHARE = NH * HD // 2
SLOTS = ((0, 0), (1, 0), (-1, 0), (0, 1), (2, 0), (1, 1), (-1, 1), (2, 1))
SLOT = {where: s for s, where in enumerate(SLOTS)}
POS = {0: 0, 1: 1, -1: 2, 2: 3}
GROUPS = ((0, 1), (1, 3), (4, 1), (5, 2), (7, 1))
SCALE2 = HD ** (-0.5) * math.log2(math.e)
BF16, F32 = jnp.bfloat16, jnp.float32


class Sems:
    def __init__(self, send, recv):
        self.send, self.recv, self.at = send, recv, {}

    def __call__(self, *name):
        index = self.at.setdefault(name, len(self.at))
        return {"send_sem": self.send.at[index], "recv_sem": self.recv.at[index]}


N_SEMS = 128


def normed(values, gains):
    factor = lax.rsqrt(jnp.mean(values * values, axis=-1, keepdims=True) + 1e-06)
    return values * factor * gains


def kernel(
    tok_hbm, wq_hbm, wo_hbm, tt_ref, wt_ref, qg_ref, kg_ref, tg_ref, out_ref,
    tok, wq, wo, kv, q, acc, top, total,
    tpart, tcr, tsum, tyr, tsum2, tzr, tkv,
    osend, orecv, ssend, srecv, att, arecv, part, precv,
    send_sems, recv_sems, local_sems,
):
    b, u = lax.axis_index("blk"), lax.axis_index("uly")
    y_lo, z, c = b // 16, (b // 2) % NZ, b % 2
    y_hi, x = u // NX, u % NX
    y = 2 * y_hi + y_lo
    sems = Sems(send_sems, recv_sems)
    pending = []

    def device(y_lo=y_lo, z=z, c=c, y_hi=y_hi, x=x):
        return {"blk": (y_lo * NZ + z) * 2 + c, "uly": y_hi * NX + x}

    def y_step(k):
        yy = (y + k) % 4
        return device(y_hi=yy // 2, y_lo=yy % 2)

    def x_step(k, o=0):
        return device(x=(x + k) % NX, y_lo=(y_lo + o) % 2)

    def z_step(k):
        return device(z=(z + k) % NZ)

    sibling = device(c=1 - c)
    partner = device(y_lo=1 - y_lo)

    def send(name, src, dst, where):
        copy = pltpu.make_async_remote_copy(
            src_ref=src, dst_ref=dst, device_id=where, device_id_type=MESH, **sems(*name)
        )
        copy.start()
        pending.append(copy)

    def wait(name, dst):
        pltpu.make_async_remote_copy(
            src_ref=dst, dst_ref=dst, device_id=sibling, device_id_type=MESH, **sems(*name)
        ).wait_recv()

    barrier = pltpu.get_barrier_semaphore()
    peers = [x_step(k, o) for k in (1, -1, 2) for o in range(2)]
    peers += [y_step(k) for k in (1, -1, 2)]
    peers += [z_step(k) for k in range(1, NZ)] + [sibling]
    for peer in peers:
        pl.semaphore_signal(barrier, inc=1, device_id=peer, device_id_type=MESH)

    def rows(start, size, step):
        return pl.ds(pl.multiple_of(start * step, step), size)

    def slot(dx, dy):
        return tok.at[SLOT[dx, dy]]

    mine = rows(y_lo, COLS, COLS)
    local_tok = pltpu.make_async_copy(tok_hbm, slot(0, 0), local_sems.at[0])
    local_wq = pltpu.make_async_copy(wq_hbm, wq, local_sems.at[1])
    local_wo = pltpu.make_async_copy(wo_hbm.at[:, mine], wo.at[0], local_sems.at[2])
    local_tok.start()
    local_wq.start()

    product = lax.dot_general(tt_ref[...], wt_ref[...], (((0,), (0,)), ((), ())), preferred_element_type=F32)
    for h in range(NH):
        for s in range(2):
            at = (2 * h + s) * HD
            tpart[s, :, h * HD:(h + 1) * HD] = product[:, at:at + HD]
    top[...] = jnp.full(top.shape, -1e30, F32)
    total[...] = jnp.zeros(total.shape, F32)
    acc[...] = jnp.zeros(acc.shape, F32)
    ssend[...] = jnp.zeros(ssend.shape, F32)

    def kv_rows(g, core):
        first, count = GROUPS[g]
        return pl.ds(pl.multiple_of(core * CHUNK + first % 4 * ROWS, ROWS), count * ROWS)

    def project(g):
        first, count = GROUPS[g]
        j = first // 4

        @pl.loop(0, NH)
        def _(h):
            columns = pl.ds(pl.multiple_of(h * 3 * HD, HD), 3 * HD)
            left = tok[first:first + count].reshape(count * ROWS, D)
            r = jnp.dot(left, wq[:, columns], preferred_element_type=F32)
            q[h, first * ROWS:(first + count) * ROWS, :] = normed(r[:, :HD], qg_ref[...]).astype(BF16)
            kv[j, z, h, kv_rows(g, c), :] = normed(r[:, HD:2 * HD], kg_ref[...]).astype(BF16)
            kv[j, z, NH + h, kv_rows(g, c), :] = r[:, 2 * HD:].astype(BF16)

    def ring_start(g):
        block = kv.at[GROUPS[g][0] // 4, z, :, kv_rows(g, c), :]
        for k in (1, -1):
            send(("kv", g, k, 1), block, block, z_step(k))

    def finish_chunk(j):
        block = kv.at[j, z, :, rows(c, CHUNK, CHUNK), :]
        send(("sib", j, 0, 0), block, block, sibling)
        own, theirs = j * CHUNK, 2 * CHUNK + j * CHUNK
        send(("q", j), q.at[:, own:own + CHUNK, :], q.at[:, theirs:theirs + CHUNK, :], partner)

    def planes(h, k):
        if h < NZ // 2:
            return pl.ds(0, 2 * NH)
        return pl.ds(0 if k == 1 else NH, NH)

    def ring(g, h):
        j = GROUPS[g][0] // 4
        for k in (1, -1):
            zz = (z - k * h) % NZ
            wait(("kv", g, k, h), kv.at[j, zz, planes(h, k), kv_rows(g, c), :])
            if h < NZ // 2:
                piece = kv.at[j, zz, planes(h + 1, k), kv_rows(g, c), :]
                send(("kv", g, k, h + 1), piece, piece, z_step(k))

    def share(j, h):
        for k in (1, -1):
            piece = kv.at[j, (z - k * h) % NZ, planes(h, k), rows(c, CHUNK, CHUNK), :]
            send(("sib", j, h, k), piece, piece, sibling)

    def await_sibling(j, h):
        for k in (1, -1) if h else (0,):
            piece = planes(h, k) if h else pl.ds(0, 2 * NH)
            wait(("sib", j, h, k), kv.at[j, (z - k * h) % NZ, piece, rows(1 - c, CHUNK, CHUNK), :])

    def attend(tiles, first=0, size=4 * CHUNK):
        at = pl.ds(first, size)
        for h in range(NH):
            pairs = tiles(h)
            scores = []
            for keys, _ in pairs:
                s = lax.dot_general(q[h, at, :], keys[...], (((1,), (1,)), ((), ())), preferred_element_type=F32)
                scores.append([s[:, i:i + HD] for i in range(0, s.shape[1], HD)])
            peak = functools.reduce(jnp.maximum, [piece for s in scores for piece in s])
            old = top[h, at, :]
            new = jnp.maximum(old, jnp.max(peak, axis=1, keepdims=True))
            shrink = jnp.exp2((old - new) * SCALE2)
            weights = [[jnp.exp2((piece - new) * SCALE2) for piece in s] for s in scores]
            total[h, at, :] = total[h, at, :] * shrink + sum(piece for w in weights for piece in w)
            blended = acc[h, at, :] * shrink
            for w, (_, values) in zip(weights, pairs):
                w = jnp.concatenate(w, axis=1).astype(BF16)
                blended = blended + jnp.dot(w, values[...], preferred_element_type=F32)
            acc[h, at, :] = blended
            top[h, at, :] = new

    def video_tiles(*where):
        def tiles(h):
            return [(kv.at[j, zz, h], kv.at[j, zz, NH + h]) for j, zz in where]

        return tiles

    local_tok.wait()
    local_wq.wait()
    local_wo.start()
    project(0)

    pl.semaphore_wait(barrier, len(peers))

    for k in (1, -1):
        send(("x", k), tok_hbm, slot(-k, 0), x_step(k))
    send(("y",), tok_hbm, slot(0, 1), y_step(2))
    ring_start(0)
    send(("tc",), tpart.at[1 - c], tcr, sibling)
    ring(0, 1)
    send(("x", 2), tok_hbm, slot(2, 0), x_step(2))

    wait(("tc",), tcr)
    tsum[...] = tpart[c] + tcr[...]
    send(("ty",), tsum.at[rows(1 - y_lo, CHUNK, CHUNK), :], tyr, partner)

    wait(("y",), slot(0, 1))
    for k in (1, -1):
        send(("yx", k), slot(0, 1), slot(-k, 1), x_step(k))
    for k in (1, -1):
        wait(("x", k), slot(-k, 0))
    project(1)
    ring_start(1)
    finish_chunk(0)
    ring(0, 2)
    wait(("x", 2), slot(2, 0))
    send(("xy",), slot(2, 0), slot(2, 1), y_step(2))
    project(2)
    ring_start(2)

    ring(0, 3)
    ring(1, 1)
    share(0, 1)
    for k in (1, -1):
        wait(("yx", k), slot(-k, 1))

    project(3)
    ring_start(3)

    for k in (1, -1):
        here = rows(c, SHARE, SHARE)
        send(("w", k), wo_hbm.at[here, mine], wo.at[POS[-k], here, :], x_step(k))
    ring(0, 4)
    ring(2, 1)

    wait(("ty",), tyr)
    tsum2[...] = tsum[rows(y_lo, CHUNK, CHUNK), :] + tyr[...]
    for dz in range(1, NZ):
        target = (z + dz) % NZ
        send(("tz", dz), tsum2.at[rows(target, HALF, HALF), :], tzr.at[dz - 1], z_step(dz))

    wait(("xy",), slot(2, 1))
    project(4)
    ring_start(4)
    finish_chunk(1)

    ring(1, 2)
    share(0, 2)
    ring(2, 2)

    for dz in range(1, NZ):
        wait(("tz", dz), tzr.at[dz - 1])
    summed = tsum2[rows(z, HALF, HALF), :]
    for dz in range(1, NZ):
        summed = summed + tzr[dz - 1]
    for h in range(NH):
        one = summed[:, h * HD:(h + 1) * HD]
        one = jnp.where(c == 0, normed(one, tg_ref[...]), one)
        tkv[c * NH + h, rows(z, HALF, HALF), :] = one.astype(BF16)

    def text_piece(dz):
        return tkv.at[pl.ds(c * NH, NH), rows((z - dz) % NZ, HALF, HALF), :]

    for dz in range(1, NZ):
        send(("tg", dz), text_piece(0), text_piece(0), z_step(dz))

    for j in range(2):
        theirs = 2 * CHUNK + j * CHUNK
        wait(("q", j), q.at[:, theirs:theirs + CHUNK, :])
    await_sibling(0, 0)
    await_sibling(1, 0)
    attend(video_tiles((0, z), (1, z)))

    def attend_far(j, h):
        await_sibling(j, h)
        attend(video_tiles((j, (z - h) % NZ), (j, (z + h) % NZ)))

    ring(3, 1)
    ring(4, 1)
    share(1, 1)
    attend_far(0, 1)
    ring(2, 3)
    ring(1, 3)
    share(0, 3)
    attend_far(0, 2)
    ring(3, 2)
    ring(4, 2)
    share(1, 2)
    attend_far(1, 1)
    ring(2, 4)
    ring(1, 4)
    share(0, 4)
    attend_far(0, 3)
    for dz in range(1, NZ):
        wait(("tg", dz), text_piece(dz))
    text_half = tkv.at[pl.ds(c * NH, NH), :, :]
    send(("ts",), text_half, text_half, sibling)

    def w_piece(dx, first=0, size=SHARE):
        return wo.at[POS[dx], pl.ds(pl.multiple_of(c * SHARE + first, SHARE // 2), size), :]

    for k, first in ((1, 0), (-1, SHARE // 2)):
        wait(("w", k), w_piece(-k))
        send(("ww", k), w_piece(-k, first, SHARE // 2), w_piece(2, first, SHARE // 2), x_step(k))
        send(("ws", -k), w_piece(-k), w_piece(-k), sibling)

    attend_far(1, 2)
    ring(3, 3)
    ring(4, 3)
    share(1, 3)
    wait(("ts",), tkv.at[pl.ds((1 - c) * NH, NH), :, :])
    attend(lambda h: [(tkv.at[h], tkv.at[NH + h])])
    await_sibling(0, 4)
    attend(video_tiles((0, (z + 4) % NZ)))
    attend_far(1, 3)
    ring(3, 4)
    ring(4, 4)
    share(1, 4)
    await_sibling(1, 4)
    last = video_tiles((1, (z + 4) % NZ))
    attend(last, 2 * CHUNK, 2 * CHUNK)

    def finished(h, at):
        weight = jnp.sum(total[h, at, :], axis=1, keepdims=True)
        return acc[h, at, :] / weight, top[h, at, :] * SCALE2 + jnp.log2(weight)

    for j in (1, 0):
        for h in range(NH):
            mean, level = finished(h, pl.ds(2 * CHUNK + j * CHUNK, CHUNK))
            osend[j, :, h * HD:(h + 1) * HD] = mean.astype(BF16)
            ssend[j, h:h + 1, :] = level.T[0:1, :]
        send(("s", j), ssend.at[j], srecv.at[j], partner)
        send(("o", j), osend.at[j], orecv.at[j], partner)

    attend(last, 0, 2 * CHUNK)

    while len(pending) > 4:
        pending.pop(0).wait_send()
    for k, first in ((1, 0), (-1, SHARE // 2)):
        wait(("ww", k), w_piece(2, first, SHARE // 2))
    send(("ws", 2), w_piece(2), w_piece(2), sibling)

    for j in (1, 0):
        wait(("s", j), srecv.at[j])
        wait(("o", j), orecv.at[j])
        for h in range(NH):
            mean, level = finished(h, pl.ds(j * CHUNK, CHUNK))
            other = jnp.broadcast_to(srecv[j, h:h + 1, :], (CHUNK, HD)).T
            peak = jnp.maximum(level, other)
            ours, theirs = jnp.exp2(level - peak), jnp.exp2(other - peak)
            both = mean * ours + orecv[j, :, h * HD:(h + 1) * HD].astype(F32) * theirs
            both = (both / (ours + theirs)).astype(BF16)
            for i in range(4):
                dx, dy = SLOTS[4 * j + i]
                att[POS[dx], dy, :, h * HD:(h + 1) * HD] = both[i * ROWS:(i + 1) * ROWS]

        for o in (1, 0):
            if j == 1:
                send(("a", 2, o), att.at[POS[2]], arecv.at[POS[2], o], x_step(2, o))
            for k in (1, -1):
                send(("a", -k, o, j), att.at[POS[k], j], arecv.at[POS[-k], o, j], x_step(k, o))
            if j == 0 and o == 1:
                send(("a", 0, o), att.at[0], arecv.at[0, o], partner)

    arecv[0, 0] = att[0]

    local_wo.wait()
    for dx in (1, -1, 2):
        wait(("ws", dx), wo.at[POS[dx], rows(1 - c, SHARE, SHARE), :])
    for o in range(2):
        for k in (1, -1):
            for j in range(2):
                wait(("a", k, o, j), arecv.at[POS[k], o, j])
        wait(("a", 2, o), arecv.at[POS[2], o])
    wait(("a", 0, 1), arecv.at[0, 1])

    away = ((1, 1), (0, 1), (1, 0))
    for half in range(2):
        for n in range(half * COLS // 2, (half + 1) * COLS // 2, 384):
            r = jnp.zeros((4 * ROWS, 384), F32)
            for p in range(NX):
                left = arecv[p].reshape(4 * ROWS, NH * HD)
                r = r + jnp.dot(left, wo[p, :, n:n + 384], preferred_element_type=F32)
            part[:, :, :, n:n + 384] = r.astype(BF16).reshape(2, 2, ROWS, 384)
        columns = pl.ds(half * COLS // 2, COLS // 2)
        for o, j in away:
            where = device(y_hi=(y_hi + j) % 2, y_lo=(y_lo + o) % 2)
            send(("p", o, j, half), part.at[o, j, :, columns], precv.at[o, j, :, columns], where)
    for half in range(2):
        for o, j in away:
            wait(("p", o, j, half), precv.at[o, j, :, pl.ds(half * COLS // 2, COLS // 2)])
    out_ref[:, rows(1 - y_lo, COLS, COLS)] = (precv[1, 0].astype(F32) + precv[1, 1].astype(F32)).astype(BF16)
    out_ref[:, mine] = (part[0, 0].astype(F32) + precv[0, 1].astype(F32)).astype(BF16)

    for copy in pending:
        copy.wait_send()


def per_device(video_tokens, w_qkv, w_out, text_tokens, w_text, q_gain, k_gain, text_gain):
    vmem, hbm = pl.BlockSpec(memory_space=pltpu.VMEM), pl.BlockSpec(memory_space=pl.ANY)
    return pl.pallas_call(
        kernel,
        out_shape=jax.ShapeDtypeStruct((ROWS, D), BF16),
        in_specs=[hbm, hbm, hbm] + [vmem] * 5,
        out_specs=vmem,
        scratch_shapes=[
            pltpu.VMEM((2 * NX, ROWS, D), BF16),
            pltpu.VMEM((D, NH * 3 * HD), BF16),
            pltpu.VMEM((NX, NH * HD, COLS), BF16),
            pltpu.VMEM((2, NZ, 2 * NH, 2 * CHUNK, HD), BF16),
            pltpu.VMEM((NH, 4 * CHUNK, HD), BF16),
            pltpu.VMEM((NH, 4 * CHUNK, HD), F32),
            pltpu.VMEM((NH, 4 * CHUNK, HD), F32),
            pltpu.VMEM((NH, 4 * CHUNK, HD), F32),
            pltpu.VMEM((2, TEXT, NH * HD), F32),
            pltpu.VMEM((TEXT, NH * HD), F32),
            pltpu.VMEM((TEXT, NH * HD), F32),
            pltpu.VMEM((CHUNK, NH * HD), F32),
            pltpu.VMEM((CHUNK, NH * HD), F32),
            pltpu.VMEM((NZ - 1, HALF, NH * HD), F32),
            pltpu.VMEM((2 * NH, CHUNK, HD), BF16),
            pltpu.VMEM((2, CHUNK, NH * HD), BF16),
            pltpu.VMEM((2, CHUNK, NH * HD), BF16),
            pltpu.VMEM((2, 8, HD), F32),
            pltpu.VMEM((2, 8, HD), F32),
            pltpu.VMEM((NX, 2, ROWS, NH * HD), BF16),
            pltpu.VMEM((NX, 2, 2, ROWS, NH * HD), BF16),
            pltpu.VMEM((2, 2, ROWS, COLS), BF16),
            pltpu.VMEM((2, 2, ROWS, COLS), BF16),
            pltpu.SemaphoreType.DMA((N_SEMS,)),
            pltpu.SemaphoreType.DMA((N_SEMS,)),
            pltpu.SemaphoreType.DMA((3,)),
        ],
        compiler_params=pltpu.CompilerParams(
            collective_id=0, has_side_effects=True, vmem_limit_bytes=56 * 1024 * 1024
        ),
        name="joint_attention",
    )(
        video_tokens, w_qkv, w_out, text_tokens.T, w_text,
        q_gain.reshape(1, HD), k_gain.reshape(1, HD), text_gain.reshape(1, HD),
    )


def solution(mesh):
    in_specs = (
        P(("blk", "uly"), None), P(None, "uly"), P("uly", None), P(None, "blk"), P("blk", "uly"), P(), P(), P(),
    )
    return jax.shard_map(
        per_device, mesh=mesh, in_specs=in_specs, out_specs=P(("blk", "uly"), None), check_vma=False
    )
```

time: 102 us -> 86.4 us (0.85); the launches traced: 102 us -> 85.5 us
  Pallas kernels: 99.1 us -> 83.8 us
  local copies, waits for them, and re-layouts: 3.15 us -> 1.62 us
    pallas_call x1, Pallas kernels: 99.1 us -> 83.8 us  [per_device(): pl.pallas_call(kernel, out_shape=jax.ShapeDtypeStruct((ROWS, D), BF16), i...]
    unnamed x2 -> x1, local copies, waits for them, and re-layouts: 3.15 us -> 1.62 us
where the time goes in v2:
time: 86.4 us; the launch traced here: 85.5 us
  Pallas kernels  83.8 us (97%)
  local copies, waits for them, and re-layouts  1.62 us (2%)
    pallas_call x1, Pallas kernels, per_device(): pl.pallas_call(kernel, out_shape=jax.ShapeDtypeStruct((ROWS, D), BF16), i...  83.8 us

profile of v2, /device:TPU:1, one launch (start us, length us, event | category | flops | bytes accessed | tf_op | source)
XLA Modules:
  0.0 85.5 jit_solution(2948373662700963862)
XLA Ops:
  0.0 83.8 %joint_attention.1 = bf16[32,3072]{1,0:T(8,128)(2,1)} custom-call(bf16[32,3072]{1,0:T(8,128)(2,1)} %tok_hbm.1, bf16[3072,1152]{1,0:T(8,128)(2,1)} %wq_hbm.1, bf16[384,3072]{1,0:T(8,128)(2,1)} %wo_hbm.1, bf16[96,256]{1,0:T(8,128)(2,1)} %bitcast.4, bf16[96,768]{1,0:T(8,128)(2,1)} %wt_ref.1, f32[1,128]{1,0:T(1,128)} %bitcast.5, f32[1,128]{1,0:T(1,128)} %bitcast.6, ...), custom_call_target="tpu_custom_call" | custom-call | tf_op jit(solution)/shard_map/joint_attention/pallas_call | solution.py:411
  83.9 1.6 %copy.10 = bf16[32,3072]{1,0:T(8,128)(2,1)} copy(bf16[32,3072]{1,0:T(8,128)(2,1)} %joint_attention.1) | data formatting | bytes 393216

commit v3 on v2

--- a/solution.py
+++ b/solution.py
@@ -105,16 +105,6 @@
     local_wo = pltpu.make_async_copy(wo_hbm.at[:, mine], wo.at[0], local_sems.at[2])
     local_tok.start()
     local_wq.start()
-
-    product = lax.dot_general(tt_ref[...], wt_ref[...], (((0,), (0,)), ((), ())), preferred_element_type=F32)
-    for h in range(NH):
-        for s in range(2):
-            at = (2 * h + s) * HD
-            tpart[s, :, h * HD:(h + 1) * HD] = product[:, at:at + HD]
-    top[...] = jnp.full(top.shape, -1e30, F32)
-    total[...] = jnp.zeros(total.shape, F32)
-    acc[...] = jnp.zeros(acc.shape, F32)
-    ssend[...] = jnp.zeros(ssend.shape, F32)
 
     def kv_rows(g, core):
         first, count = GROUPS[g]
@@ -195,19 +185,23 @@
 
         return tiles
 
+    pl.semaphore_wait(barrier, len(peers))
+
+    for k in (1, -1):
+        send(("x", k), tok_hbm, slot(-k, 0), x_step(k))
+    send(("y",), tok_hbm, slot(0, 1), y_step(2))
+
+    product = lax.dot_general(tt_ref[...], wt_ref[...], (((0,), (0,)), ((), ())), preferred_element_type=F32)
+    for h in range(NH):
+        for s in range(2):
+            at = (2 * h + s) * HD
+            tpart[s, :, h * HD:(h + 1) * HD] = product[:, at:at + HD]
+    send(("tc",), tpart.at[1 - c], tcr, sibling)
     local_tok.wait()
     local_wq.wait()
     local_wo.start()
     project(0)
-
-    pl.semaphore_wait(barrier, len(peers))
-
-    for k in (1, -1):
-        send(("x", k), tok_hbm, slot(-k, 0), x_step(k))
-    send(("y",), tok_hbm, slot(0, 1), y_step(2))
     ring_start(0)
-    send(("tc",), tpart.at[1 - c], tcr, sibling)
-    ring(0, 1)
     send(("x", 2), tok_hbm, slot(2, 0), x_step(2))
 
     wait(("tc",), tcr)
@@ -217,12 +211,27 @@
     wait(("y",), slot(0, 1))
     for k in (1, -1):
         send(("yx", k), slot(0, 1), slot(-k, 1), x_step(k))
+    ring(0, 1)
+
+    top[...] = jnp.full(top.shape, -1e30, F32)
+    total[...] = jnp.zeros(total.shape, F32)
+    acc[...] = jnp.zeros(acc.shape, F32)
+    ssend[...] = jnp.zeros(ssend.shape, F32)
+
     for k in (1, -1):
         wait(("x", k), slot(-k, 0))
     project(1)
     ring_start(1)
     finish_chunk(0)
     ring(0, 2)
+
+    wait(("ty",), tyr)
+    tsum2[...] = tsum[rows(y_lo, CHUNK, CHUNK), :] + tyr[...]
+    for dz in range(1, NZ):
+        target = (z + dz) % NZ
+        send(("tz", dz), tsum2.at[rows(target, HALF, HALF), :], tzr.at[dz - 1], z_step(dz))
+
+
     wait(("x", 2), slot(2, 0))
     send(("xy",), slot(2, 0), slot(2, 1), y_step(2))
     project(2)
@@ -242,20 +251,14 @@
         send(("w", k), wo_hbm.at[here, mine], wo.at[POS[-k], here, :], x_step(k))
     ring(0, 4)
     ring(2, 1)
-
-    wait(("ty",), tyr)
-    tsum2[...] = tsum[rows(y_lo, CHUNK, CHUNK), :] + tyr[...]
-    for dz in range(1, NZ):
-        target = (z + dz) % NZ
-        send(("tz", dz), tsum2.at[rows(target, HALF, HALF), :], tzr.at[dz - 1], z_step(dz))
+    ring(1, 2)
+    share(0, 2)
 
     wait(("xy",), slot(2, 1))
     project(4)
     ring_start(4)
     finish_chunk(1)
 
-    ring(1, 2)
-    share(0, 2)
     ring(2, 2)
 
     for dz in range(1, NZ):

time: 86.4 us -> 83.9 us (0.971)
  Pallas kernels: 83.8 us -> 82.1 us
    pallas_call x1, Pallas kernels: 83.8 us -> 82.1 us  [per_device(): pl.pallas_call(kernel, out_shape=jax.ShapeDtypeStruct((ROWS, D), BF16), i...]
where the time goes in v3:
time: 83.9 us; the launch traced here: 83.8 us
  Pallas kernels  82.1 us (98%)
  local copies, waits for them, and re-layouts  1.62 us (2%)
    pallas_call x1, Pallas kernels, per_device(): pl.pallas_call(kernel, out_shape=jax.ShapeDtypeStruct((ROWS, D), BF16), i...  82.1 us

profile of v3, /device:TPU:1, one launch (start us, length us, event | category | flops | bytes accessed | tf_op | source)
XLA Modules:
  0.0 83.8 jit_solution(5290857051840662916)
XLA Ops:
  0.0 82.1 %joint_attention.1 = bf16[32,3072]{1,0:T(8,128)(2,1)} custom-call(bf16[32,3072]{1,0:T(8,128)(2,1)} %tok_hbm.1, bf16[3072,1152]{1,0:T(8,128)(2,1)} %wq_hbm.1, bf16[384,3072]{1,0:T(8,128)(2,1)} %wo_hbm.1, bf16[96,256]{1,0:T(8,128)(2,1)} %bitcast.4, bf16[96,768]{1,0:T(8,128)(2,1)} %wt_ref.1, f32[1,128]{1,0:T(1,128)} %bitcast.5, f32[1,128]{1,0:T(1,128)} %bitcast.6, ...), custom_call_target="tpu_custom_call" | custom-call | tf_op jit(solution)/shard_map/joint_attention/pallas_call | solution.py:414
  82.1 1.6 %copy.10 = bf16[32,3072]{1,0:T(8,128)(2,1)} copy(bf16[32,3072]{1,0:T(8,128)(2,1)} %joint_attention.1) | data formatting | bytes 393216

commit v4 on v3

--- a/solution.py
+++ b/solution.py
@@ -252,6 +252,7 @@
     ring(0, 4)
     ring(2, 1)
     ring(1, 2)
+    ring(2, 2)
     share(0, 2)
 
     wait(("xy",), slot(2, 1))
@@ -259,7 +260,6 @@
     ring_start(4)
     finish_chunk(1)
 
-    ring(2, 2)
 
     for dz in range(1, NZ):
         wait(("tz", dz), tzr.at[dz - 1])
@@ -387,7 +387,7 @@
         wait(("a", 2, o), arecv.at[POS[2], o])
     wait(("a", 0, 1), arecv.at[0, 1])
 
-    away = ((1, 1), (0, 1), (1, 0))
+    away = ((0, 1), (1, 1), (1, 0))
     for half in range(2):
         for n in range(half * COLS // 2, (half + 1) * COLS // 2, 384):
             r = jnp.zeros((4 * ROWS, 384), F32)

time: 83.9 us -> 86.2 us (1.027)
  Pallas kernels: 82.1 us -> 84.4 us
    pallas_call x1, Pallas kernels: 82.1 us -> 84.4 us  [per_device(): pl.pallas_call(kernel, out_shape=jax.ShapeDtypeStruct((ROWS, D), BF16), i...]
where the time goes in v4:
time: 86.2 us; the launch traced here: 86 us
  Pallas kernels  84.4 us (98%)
  local copies, waits for them, and re-layouts  1.62 us (2%)
    pallas_call x1, Pallas kernels, per_device(): pl.pallas_call(kernel, out_shape=jax.ShapeDtypeStruct((ROWS, D), BF16), i...  84.4 us

profile of v4, /device:TPU:1, one launch (start us, length us, event | category | flops | bytes accessed | tf_op | source)
XLA Modules:
  0.0 86.0 jit_solution(1696450425830423387)
XLA Ops:
  0.0 84.4 %joint_attention.1 = bf16[32,3072]{1,0:T(8,128)(2,1)} custom-call(bf16[32,3072]{1,0:T(8,128)(2,1)} %tok_hbm.1, bf16[3072,1152]{1,0:T(8,128)(2,1)} %wq_hbm.1, bf16[384,3072]{1,0:T(8,128)(2,1)} %wo_hbm.1, bf16[96,256]{1,0:T(8,128)(2,1)} %bitcast.4, bf16[96,768]{1,0:T(8,128)(2,1)} %wt_ref.1, f32[1,128]{1,0:T(1,128)} %bitcast.5, f32[1,128]{1,0:T(1,128)} %bitcast.6, ...), custom_call_target="tpu_custom_call" | custom-call | tf_op jit(solution)/shard_map/joint_attention/pallas_call | solution.py:414
  84.4 1.6 %copy.10 = bf16[32,3072]{1,0:T(8,128)(2,1)} copy(bf16[32,3072]{1,0:T(8,128)(2,1)} %joint_attention.1) | data formatting | bytes 393216
